TPU v7x, 32 devices: a whole 2x2x4 slice. The times are simulated.
32 devices in a mesh: tmpl: 32 (over z, y, x, core), dom: 1.
Axes of the slice: x: 2, y: 2, z: 4, core: 2. Of those that a mesh axis runs over, the one named last changes fastest.
Arguments:
- particles: bfloat16 [4096, 16384], P('tmpl', 'dom'), may hold values from -8 to 8
- templates: bfloat16 [128, 18, 16384], P('tmpl', None, 'dom')
- classes: int32 [4096, 1], P('tmpl'), may hold values from 0 to 127; in each aligned block of 128 rows (0 to 127, 128 to 255, ...) at most 2 rows name the same one
- rotations: int32 [4096], P('tmpl'), may hold values from 0 to 17
Outputs:
- class_means: float32 [128, 18, 16384], P('tmpl', None, 'dom')
- weights: bfloat16 [4096], P('tmpl')
Inputs may be any that keep to these rules, and one draw needn't show every extreme that they name: `classes`: among the 128 particles of one index of tmpl (aligned blocks of rows) no class appears more than 2 times, and some class appears exactly 2 times.
All inputs are finite; a program needn't handle non-finite values.
Results may differ from a plain program's by a relative error of at most 0.0022.
Values may be sent and summed in bfloat16 or wider, within the bound.
A program may use at most 256 MiB of HBM per device.

v0:
```python
import jax
import jax.numpy as jnp
from jax import lax
from jax.sharding import PartitionSpec as P

CAPACITY = 2


eps = 1e-05


def weigh_rows(scores, class_ids, rot_ids, rot_count):
    target = class_ids * rot_count + rot_ids
    column = lax.broadcasted_iota(jnp.int32, scores.shape, 1)
    picked = jnp.sum(jnp.where(column == target[:, None], scores, 0.0), axis=1)
    mean_sq = jnp.mean(scores * scores, axis=1)
    return (picked * picked / (mean_sq + eps)).astype(jnp.bfloat16)


def body(particles, templates, classes, rotations):
    part_rows = particles.shape[0]
    pix_width = particles.shape[1]
    local_classes = templates.shape[0]
    rot_count = templates.shape[1]
    owner_count = lax.axis_size("tmpl")
    class_count = local_classes * owner_count
    all_panels = lax.all_gather(templates, "tmpl", axis=0, tiled=True)
    flat_panel = all_panels.reshape(all_panels.shape[0] * rot_count, pix_width)
    block_scores = lax.dot_general(
        particles, flat_panel, (((1,), (1,)), ((), ())), preferred_element_type=jnp.float32
    )
    class_ids = classes[:, 0]
    scores = lax.psum(block_scores, "dom")
    weights = weigh_rows(scores, class_ids, rotations, rot_count)
    row_iota = lax.broadcasted_iota(jnp.int32, (part_rows, part_rows), 0)
    col_iota = lax.broadcasted_iota(jnp.int32, (part_rows, part_rows), 1)
    same_class = (class_ids[None, :] == class_ids[:, None]) & (col_iota < row_iota)
    slot_ranks = jnp.sum(same_class.astype(jnp.int32), axis=1)
    slot_index = class_ids * CAPACITY + slot_ranks
    outgoing = (
        jnp.zeros((class_count * CAPACITY, pix_width), jnp.bfloat16).at[slot_index].set(particles)
    )
    rot_onehot = (
        lax.broadcasted_iota(jnp.int32, (part_rows, rot_count), 1) == rotations[:, None]
    ).astype(jnp.bfloat16)
    weighted_onehot = (
        jnp.zeros((class_count * CAPACITY, rot_count), jnp.bfloat16)
        .at[slot_index]
        .set(weights[:, None] * rot_onehot)
    )
    incoming, incoming_weights = (
        lax.all_to_all(outgoing, "tmpl", split_axis=0, concat_axis=0, tiled=True),
        lax.all_to_all(weighted_onehot, "tmpl", split_axis=0, concat_axis=0, tiled=True),
    )
    incoming = incoming.reshape(owner_count, local_classes, CAPACITY, pix_width)
    incoming_weights = incoming_weights.reshape(owner_count, local_classes, CAPACITY, rot_count)
    class_sums = jnp.einsum(
        "scjr,scjp->crp", incoming_weights, incoming, preferred_element_type=jnp.float32
    )
    totals = jnp.sum(incoming_weights.astype(jnp.float32), axis=(0, 2))
    class_means = class_sums / jnp.maximum(totals, 1.0)[:, :, None]
    return (class_means, weights)


def solution(mesh):
    return jax.shard_map(
        body,
        mesh=mesh,
        in_specs=(P("tmpl", "dom"), P("tmpl", None, "dom"), P("tmpl", None), P("tmpl")),
        out_specs=(P("tmpl", None, "dom"), P("tmpl")),
        check_vma=False,
    )
```

profile of v0, /device:TPU:0, one launch (start us, length us, event | category | flops | bytes accessed | tf_op | source)
XLA Modules:
  0.0 836.4 jit_solution(13802842255555588362)
XLA Ops:
  7.2 0.0 copy-start.2
  7.2 0.0 all-gather.2.cloned.1.call-start
  7.2 4.7 copy.19
  11.9 0.0 all-gather.2.cloned.1.call-update
  11.9 0.0 copy-done.2
  11.9 0.2 convert_reduce_fusion.1
  12.1 13.7 %scatter_custom_fusion.1 = bf16[256,16384]{1,0:T(8,128)(2,1)} fusion(s32[128]{0:T(128)S(1)} %fusion.11, bf16[128,16384]{1,0:T(8,128)(2,1)} %param.4, bf16[]{:T(256)} %constant.9.clone.1), kind=kCustom, calls=%fused_computation.4 | custom fusion | bytes 8389120 | tf_op jit(solution)/shard_map/scatter | solution.py:41
  25.8 0.0 copy-start
  25.8 7.5 all-to-all-start.1
  33.3 0.0 copy-done
  33.3 668.1 %all-gather.2.cloned.1.call-done = bf16[128,18,16384]{2,1,0:T(8,128)(2,1)} async-done(((bf16[4,18,16384]{2,1,0:T(8,128)(2,1)}), bf16[128,18,16384]{2,1,0:T(8,128)(2,1)}) %all-gather.2.cloned.1.call-update) | async-done | bytes 75497488 | tf_op jit(solution)/shard_map/all_gather | solution.py:27
  701.4 71.7 %reshape.36 = bf16[2304,16384]{1,0:T(8,128)(2,1)} reshape(bf16[128,18,16384]{2,1,0:T(8,128)(2,1)} %all-gather.2.cloned.1.call-done) | data formatting | bytes 150994944 | tf_op jit(solution)/shard_map/reshape | solution.py:28
  773.0 30.8 %select_reduce_fusion = (f32[128]{0:T(128)S(1)}, f32[128]{0:T(128)S(1)}) fusion(s32[128]{0:T(128)S(1)} %multiply_add_fusion, bf16[128,16384]{1,0:T(8,128)(2,1)} %param.4, bf16[2304,16384]{1,0:T(8,128)(2,1)} %reshape.36), kind=kOutput, calls=%fused_computation.7 | convolution fusion | flops 9665150976 | bytes 79693312 | tf_op jit(solution)/shard_map/dot_general | solution.py:29
  803.8 0.0 copy-start.1
  803.9 1.6 scatter_custom_fusion
  805.4 0.0 all-to-all-done.1
  805.4 2.8 all-to-all-start
  808.2 11.2 %copy.21 = bf16[32,8,16384]{2,0,1:T(8,128)(2,1)} copy(bf16[32,8,16384]{2,1,0:T(8,128)(2,1)} %all-to-all-done.1) | data formatting | bytes 16777216 | tf_op jit(solution)/shard_map/all_to_all | solution.py:52
  819.4 0.0 copy-done.1
  819.4 0.0 all-to-all-done
  819.5 0.1 copy.20
  819.6 4.7 fusion
  824.3 5.2 copy.23
  (6 shorter events, 0.1 us)
Async XLA Ops:
  7.2 4.7 copy-start.2
  7.2 694.2 %all-gather.2.cloned.1.call-start = ((), (), s32[]{:S(2)}) async-start(), calls=%async_computation.2 | async-start | bytes 103809024 | tf_op jit(solution)/shard_map/all_gather | solution.py:27
  25.8 7.5 copy-start
  25.8 779.6 %all-to-all-start.1 = ((bf16[32,8,16384]{2,1,0:T(8,128)(2,1)}), bf16[32,8,16384]{2,1,0:T(8,128)(2,1)}, u32[]{:S(2)}, u32[]{:S(2)}) async-start(bf16[32,8,16384]{2,1,0:T(8,128)(2,1)} %bitcast.22), calls=%async_computation.1 | async-start | bytes 16777216 | tf_op jit(solution)/shard_map/all_to_all | solution.py:52
  803.8 15.5 %copy-start.1 = (bf16[128]{0:T(256)(128)(2,1)}, bf16[128]{0:T(256)(128)(2,1)S(1)}, u32[]{:S(2)}) copy-start(bf16[128]{0:T(256)(128)(2,1)S(1)} %fusion.12) | copy-start | bytes 772
  805.4 14.0 %all-to-all-start = ((bf16[32,8,18]{2,1,0:T(8,128)(2,1)}), bf16[32,8,18]{2,1,0:T(8,128)(2,1)S(1)}, u32[]{:S(2)}, u32[]{:S(2)}) async-start(bf16[32,8,18]{2,1,0:T(8,128)(2,1)} %bitcast.3), calls=%async_computation | async-start | bytes 131072 | tf_op jit(solution)/shard_map/all_to_all | solution.py:53
Sparse Core Ops, SparseCore 0:
  12.0 689.2 all-gather.1
where the time goes:
time: 837 us; the launch traced here: 836 us
  waiting for transfers between devices  668 us (80%)
  local copies, waits for them, and re-layouts  107 us (13%)
  matrix products  35.5 us (4%)
  between operations  14.1 us (2%)
  starting transfers between devices  10.3 us (1%)
    all_gather x1, waiting for transfers between devices, body(): all_panels = lax.all_gather(templates, 'tmpl', axis=0, tiled=True)  668 us
    reshape x1, local copies, waits for them, and re-layouts, body(): flat_panel = all_panels.reshape(all_panels.shape[0] * rot_count, pix_width)  71.7 us
    dot_general x1, matrix products, body(): lax.dot_general(particles, flat_panel, (((1,), (1,)), ((), ())), preferre...  30.8 us
  transfers between devices with their start and end apart: 3, of which 1 were waited for; matrix products, arithmetic and copies ran while one was open for 15% of the time, Pallas kernels for 0%

commit v1 on v0

v1 whole, which is shorter than its diff:
```python
import functools

import jax
import jax.numpy as jnp
from jax import lax
from jax.experimental import pallas as pl
from jax.experimental.pallas import tpu as pltpu
from jax.sharding import PartitionSpec as P

CAPACITY = 2
CHUNKS = 4
VIA_SPAN = 1

eps = 1e-05


def place(n):
    me = lax.axis_index("tmpl")
    core = lax.rem(me, 2)
    x = lax.rem(me // 2, 2)
    y = lax.rem(me // 4, 2)
    low = lax.rem(me // 8, 2)
    high = me // 16
    return high, low, y, x, core


def index_of(high, low, y, x, core):
    return (((high * 2 + low) * 2 + y) * 2 + x) * 2 + core


def gather_kernel(n, part_ref, temp_ref, parts_ref, temps_ref, own_sem, ps_sem, pr_sem, ts_sem, tr_sem):
    highs = n // 16
    high, low, y, x, core = place(n)
    pix = part_ref.shape[1]
    width = pix // CHUNKS

    def dev(a, b, c, d, e):
        return {"tmpl": index_of(a, b, c, d, e)}

    to_low = dev(high, 1 - low, y, x, core)
    to_x = dev(high, low, y, 1 - x, core)
    to_y = dev(high, low, 1 - y, x, core)
    to_core = dev(high, low, y, x, 1 - core)
    others = [lax.rem(high + step, highs) for step in range(1, highs)]
    to_high = [dev(o, low, y, x, core) for o in others]
    came_high = [lax.rem(high + highs - step, highs) for step in range(1, highs)]

    barrier = pltpu.get_barrier_semaphore()
    peers = [to_low, to_x, to_y, to_core] + to_high
    for peer in peers:
        pl.semaphore_signal(barrier, inc=1, device_id=peer, device_id_type=pl.DeviceIdType.MESH)
    pl.semaphore_wait(barrier, len(peers))

    def cols(j):
        return pl.ds(j * width, width)

    def send(src, dst, s_sem, r_sem, peer):
        return pltpu.make_async_remote_copy(
            src_ref=src, dst_ref=dst, send_sem=s_sem, recv_sem=r_sem,
            device_id=peer, device_id_type=pl.DeviceIdType.MESH,
        )

    def part(b, d, j):
        return parts_ref.at[b, d, :, cols(j)]

    def temp(a, c, e, j):
        return temps_ref.at[a, c, e, :, cols(j)]

    y0 = highs - 1
    c0 = y0 + highs
    sent = []

    def t_send(kind, src, slot, j, peer):
        cp = send(src, temp(*slot, j), ts_sem.at[kind, j], tr_sem.at[kind, j], peer)
        cp.start()
        sent.append(cp)

    def t_wait(kind, slot, j, peer):
        send(temp(*slot, j), temp(*slot, j), ts_sem.at[kind, j], tr_sem.at[kind, j], peer).wait_recv()

    def p_send(kind, src, slot, j, peer):
        cp = send(src, part(*slot, j), ps_sem.at[kind, j], pr_sem.at[kind, j], peer)
        cp.start()
        sent.append(cp)

    def p_wait(kind, slot, j, peer):
        send(part(*slot, j), part(*slot, j), ps_sem.at[kind, j], pr_sem.at[kind, j], peer).wait_recv()

    for j in range(CHUNKS):
        own_t = temp_ref.at[:, cols(j)]
        own_p = part_ref.at[:, cols(j)]
        for i in range(highs - 1):
            t_send(i, own_t, (high, y, core), j, to_high[i])
        p_send(0, own_p, (low, x), j, to_low)
        p_send(1, own_p, (low, x), j, to_x)
        t_send(y0, own_t, (high, y, core), j, to_y)
        t_send(c0, own_t, (high, y, core), j, to_core)
    own = [
        pltpu.make_async_copy(part_ref, parts_ref.at[low, x], own_sem.at[0]),
        pltpu.make_async_copy(temp_ref, temps_ref.at[high, y, core], own_sem.at[1]),
    ]
    for cp in own:
        cp.start()

    for j in range(CHUNKS):
        for i in range(highs - 1):
            slot = (came_high[i], y, core)
            t_wait(i, slot, j, to_high[i])
            t_send(y0 + 1 + i, temp(*slot, j), slot, j, to_y)
            t_send(c0 + 1 + i, temp(*slot, j), slot, j, to_core)
        p_wait(0, (1 - low, x), j, to_low)
        if j >= VIA_SPAN:
            p_send(2, part(1 - low, x, j), (1 - low, x), j, to_x)
        p_wait(1, (low, 1 - x), j, to_x)
        if j < VIA_SPAN:
            p_send(2, part(low, 1 - x, j), (low, 1 - x), j, to_low)
        slot = (high, 1 - y, core)
        t_wait(y0, slot, j, to_y)
        t_send(c0 + highs, temp(*slot, j), slot, j, to_core)
    for j in range(CHUNKS):
        for i in range(highs - 1):
            slot = (came_high[i], 1 - y, core)
            t_wait(y0 + 1 + i, slot, j, to_y)
            t_send(c0 + highs + 1 + i, temp(*slot, j), slot, j, to_core)
    for j in range(CHUNKS):
        p_wait(2, (1 - low, 1 - x), j, to_low if j < VIA_SPAN else to_x)
        for half in range(2):
            row = y if half == 0 else 1 - y
            t_wait(c0 + half * highs, (high, row, 1 - core), j, to_core)
            for i in range(highs - 1):
                t_wait(c0 + half * highs + 1 + i, (came_high[i], row, 1 - core), j, to_core)
    for cp in own:
        cp.wait()
    for cp in sent:
        cp.wait_send()


def gather_blocks(n, particles, flat_templates):
    highs = n // 16
    rows, pix = particles.shape
    bins = flat_templates.shape[0]
    kinds = 3 * highs - 1 + highs
    total = (rows * 4 + bins * 4 * highs) * pix * 2
    return pl.pallas_call(
        functools.partial(gather_kernel, n),
        out_shape=(
            jax.ShapeDtypeStruct((2, 2, rows, pix), jnp.bfloat16),
            jax.ShapeDtypeStruct((highs, 2, 2, bins, pix), jnp.bfloat16),
        ),
        in_specs=[pl.BlockSpec(memory_space=pl.ANY)] * 2,
        out_specs=[pl.BlockSpec(memory_space=pl.ANY)] * 2,
        scratch_shapes=[
            pltpu.SemaphoreType.DMA((2,)),
            pltpu.SemaphoreType.DMA((3, CHUNKS)),
            pltpu.SemaphoreType.DMA((3, CHUNKS)),
            pltpu.SemaphoreType.DMA((kinds, CHUNKS)),
            pltpu.SemaphoreType.DMA((kinds, CHUNKS)),
        ],
        compiler_params=pltpu.CompilerParams(collective_id=0, has_side_effects=True),
        cost_estimate=pl.CostEstimate(flops=0, bytes_accessed=10 * total, transcendentals=0),
    )(particles, flat_templates)


def body(particles, templates, classes, rotations):
    rows, pix = particles.shape
    local_classes, rot_count, _ = templates.shape
    n = lax.axis_size("tmpl")
    highs = n // 16
    class_count = local_classes * n
    bins = local_classes * rot_count
    high, low, y, x, core = place(n)
    me = lax.axis_index("tmpl")

    class_ids = classes[:, 0]
    row_iota = lax.broadcasted_iota(jnp.int32, (rows, rows), 0)
    col_iota = lax.broadcasted_iota(jnp.int32, (rows, rows), 1)
    same = (class_ids[None, :] == class_ids[:, None]) & (col_iota < row_iota)
    rank = jnp.sum(same.astype(jnp.int32), axis=1)
    slot = class_ids * CAPACITY + rank
    slots = class_count * CAPACITY
    pick = (lax.broadcasted_iota(jnp.int32, (slots, rows), 0) == slot[None, :]).astype(jnp.bfloat16)
    outgoing = jnp.dot(pick, particles, preferred_element_type=jnp.float32).astype(jnp.bfloat16)
    incoming = lax.all_to_all(outgoing, "tmpl", split_axis=0, concat_axis=0, tiled=True)

    label = jnp.stack([slot, rotations], axis=0)
    labels = lax.all_gather(label, "tmpl", axis=0, tiled=False)
    all_slot, all_rot = labels[:, 0], labels[:, 1]
    all_target = (all_slot // CAPACITY) * rot_count + all_rot

    parts, temps = gather_blocks(n, particles, templates.reshape(bins, pix))
    parts = parts.reshape(4 * rows, pix)
    temps = temps.reshape(4 * highs * bins, pix)
    scores = lax.dot_general(parts, temps, (((1,), (1,)), ((), ())), preferred_element_type=jnp.float32)
    if lax.axis_size("dom") > 1:
        scores = lax.psum(scores, "dom")

    grid = all_target.reshape(highs, 2, 2, 2, 2, rows)
    grid = lax.dynamic_index_in_dim(grid, high, 0, keepdims=False)
    grid = lax.dynamic_index_in_dim(grid, y, 1, keepdims=False)
    target = lax.dynamic_index_in_dim(grid, core, 2, keepdims=False).reshape(4 * rows)
    owner = lax.broadcasted_iota(jnp.int32, (highs, 2, 2, bins), 0)
    o_y = lax.broadcasted_iota(jnp.int32, (highs, 2, 2, bins), 1)
    o_c = lax.broadcasted_iota(jnp.int32, (highs, 2, 2, bins), 2)
    o_b = lax.broadcasted_iota(jnp.int32, (highs, 2, 2, bins), 3)
    column = (index_of(owner, low, o_y, x, o_c) * bins + o_b).reshape(1, 4 * highs * bins)
    picked = jnp.sum(jnp.where(column == target[:, None], scores, 0.0), axis=1)
    square = jnp.sum(scores * scores, axis=1)
    both = jnp.stack([picked, square], axis=0)
    groups = [
        [index_of(a, b, c, d, e) for b in range(2) for d in range(2)]
        for a in range(highs) for c in range(2) for e in range(2)
    ]
    both = lax.psum(both, "tmpl", axis_index_groups=groups)
    both = lax.dynamic_index_in_dim(both.reshape(2, 4, rows), low * 2 + x, 1, keepdims=False)
    weights = (both[0] * both[0] / (both[1] / (class_count * rot_count) + eps)).astype(jnp.bfloat16)

    all_w = lax.all_gather(weights, "tmpl", axis=0, tiled=False)
    mine = local_classes * CAPACITY
    here = all_slot - me * mine
    spot = lax.broadcasted_iota(jnp.int32, (n, rows, mine), 2) == here[:, :, None]
    slot_w = jnp.sum(jnp.where(spot, all_w.astype(jnp.float32)[:, :, None], 0.0), axis=1)
    slot_r = jnp.sum(jnp.where(spot, all_rot[:, :, None], 0), axis=1)
    slot_c = lax.broadcasted_iota(jnp.int32, (n, mine), 1) // CAPACITY
    slot_bin = (slot_c * rot_count + slot_r).reshape(1, n * mine)
    bin_iota = lax.broadcasted_iota(jnp.int32, (bins, n * mine), 0)
    mix = jnp.where(bin_iota == slot_bin, slot_w.reshape(1, n * mine), 0.0)
    totals = jnp.sum(mix, axis=1)
    sums = jnp.dot(mix.astype(jnp.bfloat16), incoming, preferred_element_type=jnp.float32)
    means = sums / jnp.maximum(totals, 1.0)[:, None]
    return means.reshape(local_classes, rot_count, pix), weights


def solution(mesh):
    return jax.shard_map(
        body,
        mesh=mesh,
        in_specs=(P("tmpl", "dom"), P("tmpl", None, "dom"), P("tmpl", None), P("tmpl")),
        out_specs=(P("tmpl", None, "dom"), P("tmpl")),
        check_vma=False,
    )
```

time: 837 us -> 475 us (0.57)
  waiting for transfers between devices: 668 us -> 0.01 us
  Pallas kernels: 0 us -> 325 us
  local copies, waits for them, and re-layouts: 107 us -> 19.1 us
  blocking collectives: 0 us -> 84.6 us
  between operations: 14.1 us -> 0.9 us
    all_gather x1 -> x0, waiting for transfers between devices: 668 us -> none  [body(): all_panels = lax.all_gather(templates, 'tmpl', axis=0, tiled=True)]
    pallas_call x0 -> x1, Pallas kernels: none -> 325 us  [gather_blocks(): pl.pallas_call(functools.partial(gather_kernel, n), out_shape=(jax.ShapeD...]
    all_gather x0 -> x2, blocking collectives: none -> 77.2 us  [the longest x1 38.9 us: body(): labels = lax.all_gather(label, 'tmpl', axis=0, tiled=False)]
    reshape x1 -> x3, local copies, waits for them, and re-layouts: 71.7 us -> 7.85 us  [the longest x1 5.6 us: body(): return (means.reshape(local_classes, rot_count, pix), weights)]
    scatter x1 -> x0, local copies, waits for them, and re-layouts: 13.7 us -> none  [body(): jnp.zeros((class_count * CAPACITY, pix_width), jnp.bfloat16).at[slot_index]]
    all_to_all x2 -> x0, local copies, waits for them, and re-layouts: 11.3 us -> none  [the longest x1 11.2 us: body(): lax.all_to_all(outgoing, 'tmpl', split_axis=0, concat_axis=0, tiled=True)]
    dot_general x2 -> x3, matrix products: 35.5 us -> 33.7 us  [the longest x1 18.7 us: body(): lax.dot_general(parts, temps, (((1,), (1,)), ((), ())), preferred_element...]
  transfers between devices with their start and end apart: 3 -> 1, of which waited for: 1 -> 0; matrix products, arithmetic and copies ran while one was open for 15% -> 5% of each run, Pallas kernels for 0% -> 69%
where the time goes in v1:
time: 475 us; the launch traced here: 474 us
  Pallas kernels  325 us (68%)
  blocking collectives  84.6 us (18%)
  matrix products  33.7 us (7%)
  local copies, waits for them, and re-layouts  19.1 us (4%)
  starting transfers between devices  7.43 us (2%)
    pallas_call x1, Pallas kernels, gather_blocks(): pl.pallas_call(functools.partial(gather_kernel, n), out_shape=(jax.ShapeD...  325 us
    all_gather x1, blocking collectives, body(): labels = lax.all_gather(label, 'tmpl', axis=0, tiled=False)  38.9 us
    all_gather x1, blocking collectives, body(): all_w = lax.all_gather(weights, 'tmpl', axis=0, tiled=False)  38.3 us
    dot_general x1, matrix products, body(): lax.dot_general(parts, temps, (((1,), (1,)), ((), ())), preferred_element...  18.7 us
    unnamed x6, local copies, waits for them, and re-layouts  11 us
  transfers between devices with their start and end apart: 1, of which 0 were waited for; matrix products, arithmetic and copies ran while one was open for 5% of the time, Pallas kernels for 69%

profile of v1, /device:TPU:0, one launch (start us, length us, event | category | flops | bytes accessed | tf_op | source)
XLA Modules:
  0.0 474.2 jit_solution(9150495973108802623)
XLA Ops:
  0.6 0.9 convert_reduce_fusion
  1.5 0.7 multiply_add_fusion.2
  2.2 7.8 %fusion = bf16[32,8,16384]{2,1,0:T(8,128)(2,1)} fusion(bf16[128,16384]{1,0:T(8,128)(2,1)} %part_ref.1, s32[128]{0:T(128)S(1)} %multiply_add_fusion.2), kind=kOutput, calls=%fused_computation.1 | convolution fusion | flops 1077968896 | bytes 12583424 | tf_op jit(solution)/shard_map/dot_general | solution.py:182
  10.0 7.4 %all-to-all-start = ((bf16[32,8,16384]{2,1,0:T(8,128)(2,1)}), bf16[32,8,16384]{2,1,0:T(8,128)(2,1)}, u32[]{:S(2)}, u32[]{:S(2)}) async-start(bf16[32,8,16384]{2,1,0:T(8,128)(2,1)} %fusion), calls=%async_computation | async-start | bytes 16777216 | tf_op jit(solution)/shard_map/all_to_all | solution.py:183
  17.6 0.1 multiply_add_fusion.1
  17.6 0.1 reshape.208
  17.7 3.0 copy.12
  20.7 0.0 copy-start.1
  20.7 0.0 copy-start
  20.8 2.2 reshape.193.temp_ref
  23.0 325.2 %shard_map.59 = (bf16[2,2,128,16384]{3,2,1,0:T(8,128)(2,1)}, bf16[2,2,2,72,16384]{4,3,2,1,0:T(8,128)(2,1)}) custom-call(bf16[128,16384]{1,0:T(8,128)(2,1)} %part_ref.1, bf16[72,16384]{1,0:T(8,128)(2,1)} %reshape.193.temp_ref), custom_call_target="tpu_custom_call" | custom-call | bytes 356515840 | tf_op jit(solution)/shard_map/pallas_call | solution.py:144
  348.2 0.0 copy-done.1
  348.3 0.0 copy-done
  348.3 38.9 %all-gather.2 = s32[32,2,128]{2,1,0:T(2,128)S(1)} all-gather(s32[1,2,128]{2,1,0:T(2,128)S(1)} %add_bitcast_fusion), channel_id=2, replica_groups=mesh['tmpl'=32,'dom'=1] {'tmpl'}, dimensions={0}, use_global_device_ids=true | all-gather | bytes 33792 | tf_op jit(solution)/shard_map/all_gather | solution.py:186
  387.3 18.7 %select_reduce_fusion = (f32[512]{0:T(512)S(1)}, f32[512]{0:T(512)S(1)}) fusion(s32[512]{0:T(512)S(1)} %bitcast.39, s32[576]{0:T(1024)S(1)} %reshape.208, bf16[512,16384]{1,0:T(8,128)(2,1)} %bitcast.42, bf16[576,16384]{1,0:T(8,128)(2,1)} %bitcast.41), kind=kOutput, calls=%fused_computation.5 | convolution fusion | flops 9665150976 | bytes 35660032 | tf_op jit(solution)/shard_map/dot_general | solution.py:193
  406.0 7.4 %psum.7 = f32[2,4,128]{2,1,0:T(4,128)S(1)} all-reduce(f32[2,4,128]{2,1,0:T(4,128)S(1)} %reshape.196), channel_id=1, replica_groups={{0,2,8,10},{1,3,9,11},{4,6,12,14},{5,7,13,15},{16,18,24,26},{17,19,25,2..., use_global_device_ids=true, to_apply=%region_4.5 | all-reduce | flops 1024 | bytes 8192 | tf_op jit(solution)/shard_map/psum | solution.py:213
  413.5 38.3 %all-gather.1 = bf16[32,1,128]{2,1,0:T(2,128)(2,1)S(1)} all-gather(bf16[1,1,128]{2,1,0:T(2,128)(2,1)S(1)} %fusion.11), channel_id=3, replica_groups=mesh['tmpl'=32,'dom'=1] {'tmpl'}, dimensions={0}, use_global_device_ids=true | all-gather | bytes 8448 | tf_op jit(solution)/shard_map/all_gather | solution.py:217
  451.8 0.1 select_reduce_fusion.1
  451.9 0.1 broadcast_in_dim.54
  452.0 0.6 select_reduce_fusion.2
  452.7 0.1 reshape.198
  452.8 0.5 fusion.17
  453.3 0.1 select_reduce_fusion.3
  453.4 0.0 all-to-all-done
  453.4 7.2 %convolution_divide_fusion = f32[72,16384]{1,0:T(8,128)} fusion(bf16[32,8,16384]{2,1,0:T(8,128)(2,1)} %all-to-all-done, f32[72]{0:T(128)S(1)} %broadcast_maximum_fusion, f32[256]{0:T(256)S(1)} %broadcast_in_dim.54, s32[256]{0:T(256)S(1)} %reshape.198), kind=kOutput, calls=%fused_computation.2 | convolution fusion | flops 605196288 | bytes 13109536 | tf_op jit(solution)/shard_map/dot_general | solution.py:228
  460.6 5.6 %reshape.197 = f32[4,18,16384]{2,1,0:T(8,128)} reshape(f32[72,16384]{1,0:T(8,128)} %convolution_divide_fusion) | data formatting | bytes 9437184 | tf_op jit(solution)/shard_map/reshape | solution.py:230
  466.2 8.0 %copy.13 = f32[4,18,16384]{2,0,1:T(4,128)} copy(f32[4,18,16384]{2,1,0:T(8,128)} %reshape.197) | data formatting | bytes 9437184
  (15 shorter events, 0.2 us)
Async XLA Ops:
  10.0 443.4 %all-to-all-start = ((bf16[32,8,16384]{2,1,0:T(8,128)(2,1)}), bf16[32,8,16384]{2,1,0:T(8,128)(2,1)}, u32[]{:S(2)}, u32[]{:S(2)}) async-start(bf16[32,8,16384]{2,1,0:T(8,128)(2,1)} %fusion), calls=%async_computation | async-start | bytes 16777216 | tf_op jit(solution)/shard_map/all_to_all | solution.py:183
  20.7 327.5 %copy-start.1 = (s32[128,1]{0,1:T(1,128)S(1)}, s32[128,1]{0,1:T(1,128)}, u32[]{:S(2)}) copy-start(s32[128,1]{0,1:T(1,128)} %param.6) | copy-start | bytes 1540
  20.7 327.5 %copy-start = (s32[128]{0:T(128)S(1)}, s32[128]{0:T(128)}, u32[]{:S(2)}) copy-start(s32[128]{0:T(128)} %param.7) | copy-start | bytes 1540
